TPU v7x, 32 devices: a whole 2x2x4 slice. The times are simulated.
32 devices in a mesh: wave: 16 (over z, y, x), lev: 2 (over core).
Axes of the slice: x: 2, y: 2, z: 4, core: 2. Of those that a mesh axis runs over, the one named last changes fastest.
Arguments:
- fourier_in: bfloat16 [3, 28, 1280, 64], P(None, 'lev', 'wave'), may hold values from -6 to 6
- spectral_old: bfloat16 [3, 28, 16, 2816], P(None, 'lev', 'wave'), may hold values from -6 to 6
- legendre: bfloat16 [16, 1408, 1280], P('wave'), may hold values from -0.15625 to 0.15625
- g_matrix: float32 [28, 28], replicated, may hold values from -1 to 1
- modes_in: float32 [28, 28], replicated, may hold values from -1 to 1
- modes_out: float32 [28, 28], replicated, may hold values from -1 to 1
- mode_heating: float32 [28, 28], replicated, may hold values from -1 to 1
- mode_rates: float32 [28], replicated, may hold values from 0.1 to 10
- pair_ids: int32 [16], replicated, may hold values from 0 to 639, as said below
- lat_ids: int32 [1280], replicated, may hold values from 0 to 1279, each once
- limits: int32 [1280], replicated, may hold values from 10 to 1280
Outputs:
- spectral_new: bfloat16 [3, 28, 16, 2816], P(None, 'lev', 'wave')
- fourier_out: bfloat16 [3, 28, 1280, 64], P(None, 'lev', 'wave')
Inputs may be any that keep to these rules, and one draw needn't show every extreme that they name: `pair_ids`: distinct pair numbers. `lat_ids`: each latitude once.
All inputs are finite; a program needn't handle non-finite values.
Results may differ from a plain program's by a relative error of at most 0.018.
Values may be sent and summed in bfloat16 or wider, within the bound.
A program may use at most 64 MiB of HBM per device.

v0:
```python
import jax
import jax.numpy as jnp
from jax import lax
from jax.sharding import PartitionSpec as P

MMAX = 1280
BLOCK = 64
coupling = 2.0
highest = lax.Precision.HIGHEST


def pair_layout(pair_number, row_count):
    row_index = jnp.arange(row_count, dtype=jnp.int32)
    first_length = MMAX - pair_number
    first_pad = (first_length + BLOCK - 1) // BLOCK * BLOCK
    in_first = row_index < first_pad
    row_valid = jnp.where(
        in_first, row_index < first_length, row_index - first_pad < pair_number + 1
    )
    degree = jnp.where(
        in_first, pair_number + row_index, MMAX - 1 - pair_number + row_index - first_pad
    ).astype(jnp.float32)
    lfactor = degree * (degree + 1.0) / float(MMAX * (MMAX - 1))
    return (row_valid, lfactor, first_pad)


def level_term(matrix, vector, level_start, lev_count, row_start, row_total):
    rows_block = lax.dynamic_slice(
        matrix, (jnp.asarray(row_start, jnp.int32), level_start), (row_total, lev_count)
    )
    return jnp.dot(rows_block, vector, precision=highest, preferred_element_type=jnp.float32)


def legendre_forward(stacked, pair_table, first_pad, pair_number, row_count):
    column_count = stacked.shape[1]

    def block_step(block_index, running, which_wave):
        start_row = block_index * BLOCK
        table_rows = lax.dynamic_slice_in_dim(pair_table, start_row, BLOCK, 0)
        product = lax.dot_general(
            stacked[which_wave],
            table_rows,
            (((1,), (1,)), ((), ())),
            preferred_element_type=jnp.float32,
        )
        return lax.dynamic_update_slice_in_dim(running, product, start_row, 1)

    running = jnp.zeros((column_count, row_count), jnp.float32)
    split_block = first_pad // BLOCK
    end_block = (first_pad + pair_number + BLOCK) // BLOCK
    running = lax.fori_loop(
        0, split_block, lambda block_index, carried: block_step(block_index, carried, 0), running
    )
    running = lax.fori_loop(
        split_block,
        end_block,
        lambda block_index, carried: block_step(block_index, carried, 1),
        running,
    )
    return running


def legendre_inverse(slot_spectra, pair_table, first_pad, pair_number):
    column_count = slot_spectra.shape[0]
    lat_total = pair_table.shape[1]

    def block_step(block_index, running):
        start_row = block_index * BLOCK
        table_rows = lax.dynamic_slice_in_dim(pair_table, start_row, BLOCK, 0)
        spectra_rows = lax.dynamic_slice_in_dim(slot_spectra, start_row, BLOCK, 1)
        return running + jnp.dot(spectra_rows, table_rows, preferred_element_type=jnp.float32)

    zeros_grid = jnp.zeros((column_count, lat_total), jnp.float32)
    split_block = first_pad // BLOCK
    end_block = (first_pad + pair_number + BLOCK) // BLOCK
    first_wave = lax.fori_loop(0, split_block, block_step, zeros_grid)
    second_wave = lax.fori_loop(split_block, end_block, block_step, zeros_grid)
    return jnp.stack([first_wave, second_wave])


def body(
    fourier_in,
    spectral_old,
    legendre,
    g_matrix,
    modes_in,
    modes_out,
    mode_heating,
    mode_rates,
    pair_ids,
    lat_ids,
    limits,
):
    lev_count = fourier_in.shape[1]
    lat_count = fourier_in.shape[2]
    pair_count = legendre.shape[0]
    row_count = legendre.shape[1]
    lat_total = legendre.shape[2]
    wave_index = lax.axis_index("wave")
    level_start = lax.axis_index("lev") * lev_count
    pair_slot = 0
    pair_number = lax.dynamic_slice_in_dim(pair_ids, wave_index * pair_count + pair_slot, 1)[0]
    layouts = [(pair_number,) + pair_layout(pair_number, row_count)]
    own_lats = lax.dynamic_slice_in_dim(lat_ids, wave_index * lat_count, lat_count)
    matches = own_lats[:, None] == jnp.arange(lat_total, dtype=jnp.int32)[None, :]
    row_limit = jnp.sum(jnp.where(matches, limits[None, :], 0), axis=1)
    both_waves = jnp.stack([pair_ids, MMAX - 1 - pair_ids], axis=1)
    column_wave = jnp.repeat(both_waves, 2, axis=1).reshape(-1)
    keep_mask = column_wave[None, :] < row_limit[:, None]
    masked = jnp.where(keep_mask[None, None], fourier_in, jnp.zeros((), fourier_in.dtype))
    exchanged = lax.all_to_all(masked, "wave", split_axis=3, concat_axis=2, tiled=True)
    item_count = exchanged.shape[0]
    column_count = item_count * lev_count * 2
    pair_slot = 0
    pair_number, row_valid, lfactor, first_pad = layouts[pair_slot]
    slot_data = exchanged.reshape(item_count, lev_count, lat_total, 2, 2)
    stacked = jnp.transpose(slot_data, (3, 0, 1, 4, 2)).reshape(2, column_count, lat_total)
    spectra = legendre_forward(stacked, legendre[pair_slot], first_pad, pair_number, row_count)
    spectra = jnp.where(row_valid[None, :], spectra, 0.0)
    results = [spectra.reshape(item_count, lev_count, 2, row_count)]
    tendency = jnp.stack(results, axis=2)
    flat_size = pair_count * 2 * row_count
    old_fields = spectral_old.reshape(3, lev_count, pair_count, 2, row_count).astype(jnp.float32)
    vorticity = (old_fields[0] + tendency[0]).reshape(lev_count, flat_size)
    divergence = (old_fields[1] + tendency[1]).reshape(lev_count, flat_size)
    heat_star = (old_fields[2] + tendency[2]).reshape(lev_count, flat_size)
    wave_factor = jnp.stack(
        [jnp.broadcast_to(layout[2][None, :], (2, row_count)) for layout in layouts]
    ).reshape(1, flat_size)
    keep_rows = jnp.stack(
        [jnp.broadcast_to(layout[1][None, :], (2, row_count)) for layout in layouts]
    ).reshape(1, flat_size)
    rates_own = lax.dynamic_slice_in_dim(mode_rates, level_start, lev_count)
    hydrostatic = lax.psum_scatter(
        level_term(
            g_matrix,
            heat_star,
            level_start,
            lev_count,
            jnp.int32(0),
            lev_count * lax.axis_size("lev"),
        ).astype(jnp.bfloat16),
        "lev",
        scatter_dimension=0,
        tiled=True,
    ).astype(jnp.float32)
    right_own = divergence + coupling * wave_factor * hydrostatic
    projected = lax.psum_scatter(
        level_term(
            modes_in,
            right_own,
            level_start,
            lev_count,
            jnp.int32(0),
            lev_count * lax.axis_size("lev"),
        ).astype(jnp.bfloat16),
        "lev",
        scatter_dimension=0,
        tiled=True,
    ).astype(jnp.float32)
    modal_part = projected / (1.0 + coupling * coupling * wave_factor * rates_own[:, None])
    row_start = jnp.int32(0)
    row_total = lev_count * lax.axis_size("lev")
    divergence_part = level_term(
        modes_out, modal_part, level_start, lev_count, row_start, row_total
    )
    heating_part = level_term(
        mode_heating, modal_part, level_start, lev_count, row_start, row_total
    )
    rebuilt = lax.psum_scatter(
        jnp.stack([divergence_part, heating_part], axis=1).astype(jnp.bfloat16),
        "lev",
        scatter_dimension=0,
        tiled=True,
    ).astype(jnp.float32)
    vorticity_out = jnp.where(keep_rows, vorticity, 0.0).astype(jnp.bfloat16)
    divergence_out = jnp.where(keep_rows, rebuilt[:, 0], 0.0).astype(jnp.bfloat16)
    heat_out = jnp.where(keep_rows, heat_star - coupling * rebuilt[:, 1], 0.0).astype(jnp.bfloat16)
    spectral_new = jnp.stack([vorticity_out, divergence_out, heat_out]).reshape(
        3, lev_count, pair_count, 2 * row_count
    )
    pair_slot = 0
    pair_number, row_valid, lfactor, first_pad = layouts[pair_slot]
    slot_spectra = spectral_new[:, :, pair_slot].reshape(3 * lev_count * 2, row_count)
    grid_part = legendre_inverse(slot_spectra, legendre[pair_slot], first_pad, pair_number)
    grid_part = (
        grid_part.reshape(2, 3, lev_count, 2, lat_total)
        .transpose(1, 2, 4, 0, 3)
        .reshape(3, lev_count, lat_total, 4)
    )
    gridded = grid_part.astype(jnp.bfloat16)
    returned = lax.all_to_all(gridded, "wave", split_axis=2, concat_axis=3, tiled=True)
    fourier_out = jnp.where(keep_mask[None, None], returned, jnp.zeros((), jnp.bfloat16))
    return (spectral_new, fourier_out)


def solution(mesh):
    placed = (
        P(None, "lev", "wave", None),
        P(None, "lev", "wave", None),
        P("wave", None, None),
        P(),
        P(),
        P(),
        P(),
        P(),
        P(),
        P(),
        P(),
    )
    return jax.shard_map(
        body,
        mesh=mesh,
        in_specs=placed,
        out_specs=(P(None, "lev", "wave", None), P(None, "lev", "wave", None)),
        check_vma=False,
    )
```

profile of v0, /device:TPU:0, one launch (start us, length us, event | category | flops | bytes accessed | tf_op | source)
XLA Modules:
  0.0 189.5 jit_solution(12464096708221175484)
XLA Ops:
  9.6 0.9 select_reduce_fusion
  10.6 1.2 broadcast_select_fusion.1
  11.8 1.3 copy.81
  13.1 8.3 %all-to-all-start = ((bf16[3,14,80,64]{2,1,0,3:T(8,128)(2,1)}), bf16[3,14,80,64]{2,1,0,3:T(8,128)(2,1)S(1)}, u32[]{:S(2)}, u32[]{:S(2)}) async-start(bf16[3,14,80,64]{2,1,0,3:T(8,128)(2,1)} %copy.81), calls=%async_computation | async-start | bytes 1572864 | tf_op jit(solution)/shard_map/all_to_all | solution.py:111
  25.5 15.7 %all-to-all-done = bf16[3,14,80,64]{2,1,0,3:T(8,128)(2,1)S(1)} async-done(((bf16[3,14,80,64]{2,1,0,3:T(8,128)(2,1)}), bf16[3,14,80,64]{2,1,0,3:T(8,128)(2,1)S(1)}, u32[]{:S(2)}, u32[]{:S(2)}) %all-to-all-start) | async-done | bytes 430112 | tf_op jit(solution)/shard_map/all_to_all | solution.py:111
  41.7 1.1 reshape.292
  43.2 19.2 %while.40 = (s32[]{:T(128)}, f32[84,1408]{0,1:T(8,128)S(1)}, s32[]{:T(128)}, bf16[1408,1280]{1,0:T(8,128)(2,1)}, bf16[2,84,1280]{2,1,0:T(8,128)(2,1)S(1)}, /*index=5*/s32[]{:T(128)}, s32[]{:T(128)}, s32[]{:T(128)}, s32[]{:T(128)}) while((s32[]{:T(128)}, f32[84,1408]{0,1:T(8,128)S(1)}, s32[]{:T(128)}, bf16[1408,1280]{1,0:T(8,128)(2,1)}, ...), condition=%wide.region_2.3_spmd, body=%wide.region_1.2_spmd.sunk | while | flops 13762566 | bytes 423051 | solution.py:51
  43.2 1.1 fusion.76
  44.3 1.1 fusion.76
  45.5 1.1 fusion.76
  46.6 1.1 fusion.76
  47.7 1.1 fusion.76
  48.9 1.1 fusion.76
  50.0 1.1 fusion.76
  51.1 1.1 fusion.76
  52.3 1.1 fusion.76
  53.4 1.1 fusion.76
  54.5 1.1 fusion.76
  55.7 1.1 fusion.76
  56.8 1.1 fusion.76
  57.9 1.1 fusion.76
  59.1 1.1 fusion.76
  60.2 1.1 fusion.76
  61.3 1.1 fusion.76
  62.4 4.5 %while.41 = (s32[]{:T(128)}, f32[84,1408]{0,1:T(8,128)S(1)}, s32[]{:T(128)}, bf16[1408,1280]{1,0:T(8,128)(2,1)}, bf16[2,84,1280]{2,1,0:T(8,128)(2,1)S(1)}, /*index=5*/s32[]{:T(128)}, s32[]{:T(128)}, s32[]{:T(128)}, s32[]{:T(128)}) while((s32[]{:T(128)}, f32[84,1408]{0,1:T(8,128)S(1)}, s32[]{:T(128)}, bf16[1408,1280]{1,0:T(8,128)(2,1)}, ...), condition=%wide.region_4.5_spmd, body=%wide.region_3.4_spmd.sunk | while | flops 13762566 | bytes 423051 | solution.py:54
  62.5 1.1 fusion.79
  63.6 1.1 fusion.79
  64.7 1.1 fusion.79
  65.9 1.1 fusion.79
  68.6 3.0 %fusion = bf16[16,2816]{1,0:T(8,128)(2,1)S(1)} fusion(bf16[28,2816]{1,0:T(8,128)(2,1)S(1)} %convolution_convert_fusion.3), kind=kCustom, calls=%all-reduce-scatter | all-reduce-scatter fusion | flops 90113 | bytes 248320
  71.6 2.3 %collective-permute-start = (bf16[2,2816]{1,0:T(2,128)(2,1)S(1)}, bf16[2,2816]{1,0:T(2,128)(2,1)S(1)}, u32[]{:S(2)}, u32[]{:S(2)}) collective-permute-start(bf16[2,2816]{1,0:T(2,128)(2,1)S(1)} %slice.52), channel_id=1, source_target_pairs={{0,1},{2,3},{4,5},{6,7},{8,9},{10,11},{12,13},{14,15},{16,17},{18,... | collective-permute-start | bytes 33800
  76.9 3.0 %fusion.1 = bf16[16,2816]{1,0:T(8,128)(2,1)S(1)} fusion(bf16[28,2816]{1,0:T(8,128)(2,1)S(1)} %convolution_convert_fusion.2), kind=kCustom, calls=%all-reduce-scatter.1 | all-reduce-scatter fusion | flops 90113 | bytes 248320
  80.0 2.3 %collective-permute-start.1 = (bf16[2,2816]{1,0:T(2,128)(2,1)S(1)}, bf16[2,2816]{1,0:T(2,128)(2,1)S(1)}, u32[]{:S(2)}, u32[]{:S(2)}) collective-permute-start(bf16[2,2816]{1,0:T(2,128)(2,1)S(1)} %slice.53), channel_id=1, source_target_pairs={{0,1},{2,3},{4,5},{6,7},{8,9},{10,11},{12,13},{14,15},{16,17},{18,... | collective-permute-start | bytes 33800
  84.4 1.0 copy.89
  86.6 16.7 %all-reduce.7.cloned.1.call-done = bf16[28,2,2816]{2,1,0:T(2,128)(2,1)} async-done(((bf16[28,2,2816]{2,1,0:T(2,128)(2,1)}), bf16[28,2,2816]{2,1,0:T(2,128)(2,1)}) %all-reduce.7.cloned.1.call-update) | async-done | bytes 315408
  103.3 1.0 constant_dynamic-slice_fusion
  105.4 4.9 %while.43 = (s32[]{:T(128)}, f32[84,1280]{1,0:T(8,128)S(1)}, s32[]{:T(128)}, bf16[84,1408]{1,0:T(8,128)(2,1)S(1)}, bf16[1408,1280]{1,0:T(8,128)(2,1)}, /*index=5*/s32[]{:T(128)}, s32[]{:T(128)}, s32[]{:T(128)}, s32[]{:T(128)}) while((s32[]{:T(128)}, f32[84,1280]{1,0:T(8,128)S(1)}, s32[]{:T(128)}, bf16[84,1408]{1,0:T(8,128)(2,1)S(1)}, ...), condition=%wide.region_11.12_spmd, body=%wide.region_10.11_spmd.sunk | while | flops 13870086 | bytes 1068171 | solution.py:77
  105.4 1.2 convolution_add_fusion.5
  106.6 1.2 convolution_add_fusion.5
  107.8 1.2 convolution_add_fusion.5
  109.1 1.2 convolution_add_fusion.5
  110.4 20.7 %while.42 = (s32[]{:T(128)}, f32[84,1280]{1,0:T(8,128)S(1)}, s32[]{:T(128)}, bf16[84,1408]{1,0:T(8,128)(2,1)S(1)}, bf16[1408,1280]{1,0:T(8,128)(2,1)}, /*index=5*/s32[]{:T(128)}, s32[]{:T(128)}, s32[]{:T(128)}, s32[]{:T(128)}) while((s32[]{:T(128)}, f32[84,1280]{1,0:T(8,128)S(1)}, s32[]{:T(128)}, bf16[84,1408]{1,0:T(8,128)(2,1)S(1)}, ...), condition=%wide.region_9.10_spmd, body=%wide.region_8.9_spmd.sunk | while | flops 13870086 | bytes 1068171 | solution.py:76
  110.5 1.2 convolution_add_fusion.4
  111.7 1.2 convolution_add_fusion.4
  112.9 1.2 convolution_add_fusion.4
  114.1 1.2 convolution_add_fusion.4
  115.3 1.2 convolution_add_fusion.4
  116.6 1.2 convolution_add_fusion.4
  117.8 1.2 convolution_add_fusion.4
  119.0 1.2 convolution_add_fusion.4
  120.2 1.2 convolution_add_fusion.4
  121.4 1.2 convolution_add_fusion.4
  122.6 1.2 convolution_add_fusion.4
  123.9 1.2 convolution_add_fusion.4
  125.1 1.2 convolution_add_fusion.4
  126.3 1.2 convolution_add_fusion.4
  127.5 1.2 convolution_add_fusion.4
  128.7 1.2 convolution_add_fusion.4
  129.9 1.2 convolution_add_fusion.4
  131.9 6.4 %copy.98 = bf16[3,14,1280,2,2]{1,4,3,0,2:T(2,128)(2,1)} copy(bf16[3,14,1280,2,2]{2,4,3,1,0:T(2,128)(2,1)S(1)} %maximum_bitcast_fusion) | data formatting | bytes 860160 | tf_op jit(solution)/shard_map/convert_element_type | solution.py:191
  138.3 6.7 %reshape.298 = bf16[16,2,6720]{2,1,0:T(2,128)(2,1)S(1)} reshape(bf16[1280,3,4,14]{3,2,1,0:T(4,128)(2,1)} %bitcast.96) | data formatting | bytes 860160
  145.0 20.5 %all_to_all.33 = bf16[16,2,6720]{2,1,0:T(2,128)(2,1)S(1)} all-to-all(bf16[16,2,6720]{2,1,0:T(2,128)(2,1)S(1)} %reshape.298), channel_id=1, replica_groups=mesh['wave'=16,'lev'=2] {'wave'}, dimensions={0} | all-to-all | bytes 860160 | tf_op jit(solution)/shard_map/all_to_all | solution.py:192
  165.5 10.5 %reshape.299 = bf16[1280,3,4,14]{3,2,1,0:T(4,128)(2,1)} reshape(bf16[16,2,6720]{2,1,0:T(2,128)(2,1)S(1)} %all_to_all.33) | data formatting | bytes 860160
  175.9 5.5 %copy.99 = bf16[3,14,16,80,4]{3,2,4,1,0:T(8,128)(2,1)S(1)} copy(bf16[3,14,16,80,4]{1,4,0,3,2:T(4,128)(2,1)} %bitcast.97) | data formatting | bytes 860160 | tf_op jit(solution)/shard_map/all_to_all | solution.py:192
  (75 shorter events, 13.6 us)
Async XLA Ops:
  7.2 60.9 %copy-start = (f32[28,28]{1,0:T(8,128)S(1)}, f32[28,28]{1,0:T(8,128)}, u32[]{:S(2)}) copy-start(f32[28,28]{1,0:T(8,128)} %param.22) | copy-start | bytes 9412
  7.2 14.3 %copy-start.4 = (s32[16]{0:T(128)S(1)}, s32[16]{0:T(128)}, u32[]{:S(2)}) copy-start(s32[16]{0:T(128)} %param.27) | copy-start | bytes 196
  7.2 18.2 %copy-start.1 = (bf16[3,14,1,2816]{3,1,2,0:T(8,128)(2,1)S(1)}, bf16[3,14,1,2816]{3,1,2,0:T(8,128)(2,1)}, u32[]{:S(2)}) copy-start(bf16[3,14,1,2816]{3,1,2,0:T(8,128)(2,1)} %param.20) | copy-start | bytes 709636
  13.1 28.1 %all-to-all-start = ((bf16[3,14,80,64]{2,1,0,3:T(8,128)(2,1)}), bf16[3,14,80,64]{2,1,0,3:T(8,128)(2,1)S(1)}, u32[]{:S(2)}, u32[]{:S(2)}) async-start(bf16[3,14,80,64]{2,1,0,3:T(8,128)(2,1)} %copy.81), calls=%async_computation | async-start | bytes 1572864 | tf_op jit(solution)/shard_map/all_to_all | solution.py:111
  21.5 81.9 %all-reduce.7.cloned.1.call-start = ((), (), s32[]{:S(2)}) async-start(), calls=%async_computation.2 | async-start | bytes 630784
  67.0 7.6 %copy-start.3 = (u32[32]{0:T(128)S(1)}, u32[32]{0:T(128)}, u32[]{:S(2)}) copy-start(u32[32]{0:T(128)} %constant.117) | copy-start | bytes 388
  67.2 9.2 %copy-start.2 = (f32[28,28]{1,0:T(8,128)S(1)}, f32[28,28]{1,0:T(8,128)}, u32[]{:S(2)}) copy-start(f32[28,28]{1,0:T(8,128)} %param.23) | copy-start | bytes 9412
  67.3 15.0 %copy-start.7 = (f32[28]{0:T(128)S(1)}, f32[28]{0:T(128)}, u32[]{:S(2)}) copy-start(f32[28]{0:T(128)} %param.26) | copy-start | bytes 340
  67.3 16.1 %copy-start.5 = (f32[28,28]{1,0:T(8,128)S(1)}, f32[28,28]{1,0:T(8,128)}, u32[]{:S(2)}) copy-start(f32[28,28]{1,0:T(8,128)} %param.25) | copy-start | bytes 9412
  67.7 16.1 %copy-start.6 = (f32[28,28]{1,0:T(8,128)S(1)}, f32[28,28]{1,0:T(8,128)}, u32[]{:S(2)}) copy-start(f32[28,28]{1,0:T(8,128)} %param.24) | copy-start | bytes 9412
  71.6 4.5 %collective-permute-start = (bf16[2,2816]{1,0:T(2,128)(2,1)S(1)}, bf16[2,2816]{1,0:T(2,128)(2,1)S(1)}, u32[]{:S(2)}, u32[]{:S(2)}) collective-permute-start(bf16[2,2816]{1,0:T(2,128)(2,1)S(1)} %slice.52), channel_id=1, source_target_pairs={{0,1},{2,3},{4,5},{6,7},{8,9},{10,11},{12,13},{14,15},{16,17},{18,... | collective-permute-start | bytes 33800
  80.0 3.1 %collective-permute-start.1 = (bf16[2,2816]{1,0:T(2,128)(2,1)S(1)}, bf16[2,2816]{1,0:T(2,128)(2,1)S(1)}, u32[]{:S(2)}, u32[]{:S(2)}) collective-permute-start(bf16[2,2816]{1,0:T(2,128)(2,1)S(1)} %slice.53), channel_id=1, source_target_pairs={{0,1},{2,3},{4,5},{6,7},{8,9},{10,11},{12,13},{14,15},{16,17},{18,... | collective-permute-start | bytes 33800
Sparse Core Ops, SparseCore 0:
  85.6 17.6 all-reduce.6
where the time goes:
time: 191 us; the launch traced here: 190 us
  matrix products  50.2 us (26%)
  local copies, waits for them, and re-layouts  39.6 us (21%)
  waiting for transfers between devices  33.2 us (17%)
  blocking collectives  26.5 us (14%)
  between operations  19.2 us (10%)
  starting transfers between devices  12.9 us (7%)
  other arithmetic  6.88 us (4%)
    dot_general x21, matrix products, block_step(): jnp.dot(spectra_rows, table_rows, preferred_element_type=jnp.float32)  25 us
    dot_general x21, matrix products, block_step(): lax.dot_general(stacked[which_wave], table_rows, (((1,), (1,)), ((), ()))...  23.2 us
    all_to_all x1, blocking collectives, body(): lax.all_to_all(gridded, 'wave', split_axis=2, concat_axis=3, tiled=True)  20.5 us
    unnamed x24, local copies, waits for them, and re-layouts  19.4 us
    unnamed x4, waiting for transfers between devices  17.5 us
    all_to_all x1, waiting for transfers between devices, body(): lax.all_to_all(masked, 'wave', split_axis=3, concat_axis=2, tiled=True)  15.7 us
    all_to_all x1, starting transfers between devices, body(): lax.all_to_all(masked, 'wave', split_axis=3, concat_axis=2, tiled=True)  8.3 us
    convert_element_type x1, local copies, waits for them, and re-layouts, body(): gridded = grid_part.astype(jnp.bfloat16)  6.42 us
  transfers between devices with their start and end apart: 4, of which 3 were waited for; matrix products, arithmetic and copies ran while one was open for 1% of the time, Pallas kernels for 0%

commit v1 on v0

--- a/solution.py
+++ b/solution.py
@@ -7,6 +7,18 @@
 BLOCK = 64
 coupling = 2.0
 highest = lax.Precision.HIGHEST
+
+
+def trees_arrange(vals, array_axis, mine_x):
+    state_next, after = (vals.shape[:array_axis], vals.shape[array_axis + 1 :])
+    y1 = vals.reshape(*state_next, mine_x, -1, *after)
+    return jnp.moveaxis(y1, array_axis, 0)
+
+
+def touch_view(original, ndim_at):
+    h_now = list(original.shape[1:])
+    h_now[ndim_at] *= original.shape[0]
+    return jnp.moveaxis(original, 0, ndim_at).reshape(h_now)
 
 
 def pair_layout(pair_number, row_count):
@@ -189,7 +201,22 @@
         .reshape(3, lev_count, lat_total, 4)
     )
     gridded = grid_part.astype(jnp.bfloat16)
-    returned = lax.all_to_all(gridded, "wave", split_axis=2, concat_axis=3, tiled=True)
+
+    def cycles_attach(local_block, raw, axis_name, x_in):
+        local_out = lax.psum(1, axis_name=axis_name)
+        formed = lax.axis_index(axis_name)
+        met_up, block_out = (local_out, formed)
+        even = trees_arrange(local_block, x_in, met_up)
+        inbox = [even[block_out]]
+        for i in [*range(1, met_up)]:
+            row_out = even[block_out ^ i]
+            y = lax.ppermute(row_out, axis_name=axis_name, perm=[(p, p ^ i) for p in range(met_up)])
+            inbox.append(y)
+        all_values = jnp.stack(inbox, axis=0)
+        even = all_values[block_out ^ jnp.arange(met_up)]
+        return touch_view(even, raw)
+
+    returned = cycles_attach(gridded, 3, "wave", 2)
     fourier_out = jnp.where(keep_mask[None, None], returned, jnp.zeros((), jnp.bfloat16))
     return (spectral_new, fourier_out)
 

time: 191 us -> 181 us (0.948)
  starting transfers between devices: 12.9 us -> 40.3 us
  local copies, waits for them, and re-layouts: 39.6 us -> 14.9 us
  blocking collectives: 26.5 us -> 5.99 us
  waiting for transfers between devices: 33.2 us -> 40.3 us
    ppermute x0 -> x15, starting transfers between devices: none -> 27.4 us  [cycles_attach(): lax.ppermute(row_out, axis_name=axis_name, perm=[(p, p ^ i) for p in rang...]
    all_to_all x1 -> x0, blocking collectives: 20.5 us -> none  [body(): lax.all_to_all(gridded, 'wave', split_axis=2, concat_axis=3, tiled=True)]
    unnamed x24 -> x52, local copies, waits for them, and re-layouts: 19.4 us -> 2.9 us
    ppermute x0 -> x15, waiting for transfers between devices: none -> 7.3 us  [cycles_attach(): lax.ppermute(row_out, axis_name=axis_name, perm=[(p, p ^ i) for p in rang...]
    all_to_all x2 -> x0, local copies, waits for them, and re-layouts: 5.79 us -> none  [body(): lax.all_to_all(gridded, 'wave', split_axis=2, concat_axis=3, tiled=True)]
    convert_element_type x1, local copies, waits for them, and re-layouts: 6.42 us -> 0.82 us  [body(): gridded = grid_part.astype(jnp.bfloat16)]
  transfers between devices with their start and end apart: 4 -> 19, of which waited for: 3 -> 6; matrix products, arithmetic and copies ran while one was open for 1% -> 2% of each run, Pallas kernels for 0% -> 0%
where the time goes in v1:
time: 181 us; the launch traced here: 179 us
  matrix products  50.2 us (28%)
  starting transfers between devices  40.3 us (22%)
  waiting for transfers between devices  40.3 us (22%)
  between operations  19.5 us (11%)
  local copies, waits for them, and re-layouts  14.9 us (8%)
  other arithmetic  6.9 us (4%)
  blocking collectives  5.99 us (3%)
    ppermute x15, starting transfers between devices, cycles_attach(): lax.ppermute(row_out, axis_name=axis_name, perm=[(p, p ^ i) for p in rang...  27.4 us
    dot_general x21, matrix products, block_step(): jnp.dot(spectra_rows, table_rows, preferred_element_type=jnp.float32)  25 us
    dot_general x21, matrix products, block_step(): lax.dot_general(stacked[which_wave], table_rows, (((1,), (1,)), ((), ()))...  23.2 us
    unnamed x4, waiting for transfers between devices  17.3 us
    all_to_all x1, waiting for transfers between devices, body(): lax.all_to_all(masked, 'wave', split_axis=3, concat_axis=2, tiled=True)  15.7 us
    all_to_all x1, starting transfers between devices, body(): lax.all_to_all(masked, 'wave', split_axis=3, concat_axis=2, tiled=True)  8.3 us
    ppermute x15, waiting for transfers between devices, cycles_attach(): lax.ppermute(row_out, axis_name=axis_name, perm=[(p, p ^ i) for p in rang...  7.3 us
    unnamed x2, blocking collectives  5.99 us
  transfers between devices with their start and end apart: 19, of which 6 were waited for; matrix products, arithmetic and copies ran while one was open for 2% of the time, Pallas kernels for 0%

profile of v1, /device:TPU:0, one launch (start us, length us, event | category | flops | bytes accessed | tf_op | source)
XLA Modules:
  0.0 179.4 jit_solution(2642428775145617123)
XLA Ops:
  10.6 1.2 broadcast_select_fusion.1
  11.8 1.4 copy.61
  13.2 8.3 %all-to-all-start = ((bf16[3,14,80,64]{2,1,0,3:T(8,128)(2,1)}), bf16[3,14,80,64]{2,1,0,3:T(8,128)(2,1)S(1)}, u32[]{:S(2)}, u32[]{:S(2)}) async-start(bf16[3,14,80,64]{2,1,0,3:T(8,128)(2,1)} %copy.61), calls=%async_computation | async-start | bytes 1572864 | tf_op jit(solution)/shard_map/all_to_all | solution.py:123
  25.5 15.7 %all-to-all-done = bf16[3,14,80,64]{2,1,0,3:T(8,128)(2,1)S(1)} async-done(((bf16[3,14,80,64]{2,1,0,3:T(8,128)(2,1)}), bf16[3,14,80,64]{2,1,0,3:T(8,128)(2,1)S(1)}, u32[]{:S(2)}, u32[]{:S(2)}) %all-to-all-start) | async-done | bytes 430112 | tf_op jit(solution)/shard_map/all_to_all | solution.py:123
  43.2 19.2 %while.40 = (s32[]{:T(128)}, f32[84,1408]{0,1:T(8,128)S(1)}, s32[]{:T(128)}, bf16[1408,1280]{1,0:T(8,128)(2,1)}, bf16[2,84,1280]{2,1,0:T(8,128)(2,1)S(1)}, /*index=5*/s32[]{:T(128)}, s32[]{:T(128)}, s32[]{:T(128)}, s32[]{:T(128)}) while((s32[]{:T(128)}, f32[84,1408]{0,1:T(8,128)S(1)}, s32[]{:T(128)}, bf16[1408,1280]{1,0:T(8,128)(2,1)}, ...), condition=%wide.region_2.3_spmd, body=%wide.region_1.2_spmd.sunk | while | flops 13762566 | bytes 423059 | solution.py:63
  43.2 1.1 fusion.77
  44.4 1.1 fusion.77
  45.5 1.1 fusion.77
  46.6 1.1 fusion.77
  47.7 1.1 fusion.77
  50.0 1.1 fusion.77
  51.1 1.1 fusion.77
  53.4 1.1 fusion.77
  54.5 1.1 fusion.77
  56.8 1.1 fusion.77
  57.9 1.1 fusion.77
  60.2 1.1 fusion.77
  61.3 1.1 fusion.77
  62.4 4.5 %while.41 = (s32[]{:T(128)}, f32[84,1408]{0,1:T(8,128)S(1)}, s32[]{:T(128)}, bf16[1408,1280]{1,0:T(8,128)(2,1)}, bf16[2,84,1280]{2,1,0:T(8,128)(2,1)S(1)}, /*index=5*/s32[]{:T(128)}, s32[]{:T(128)}, s32[]{:T(128)}, s32[]{:T(128)}) while((s32[]{:T(128)}, f32[84,1408]{0,1:T(8,128)S(1)}, s32[]{:T(128)}, bf16[1408,1280]{1,0:T(8,128)(2,1)}, ...), condition=%wide.region_4.5_spmd, body=%wide.region_3.4_spmd.sunk | while | flops 13762566 | bytes 423059 | solution.py:66
  64.7 1.1 fusion.80
  65.9 1.1 fusion.80
  68.6 3.0 %fusion = bf16[16,2816]{1,0:T(8,128)(2,1)S(1)} fusion(bf16[28,2816]{1,0:T(8,128)(2,1)S(1)} %convolution_convert_fusion.3), kind=kCustom, calls=%all-reduce-scatter | all-reduce-scatter fusion | flops 90113 | bytes 248320
  71.6 2.3 %collective-permute-start.15 = (bf16[2,2816]{1,0:T(2,128)(2,1)S(1)}, bf16[2,2816]{1,0:T(2,128)(2,1)S(1)}, u32[]{:S(2)}, u32[]{:S(2)}) collective-permute-start(bf16[2,2816]{1,0:T(2,128)(2,1)S(1)} %slice.54), channel_id=1, source_target_pairs={{0,1},{2,3},{4,5},{6,7},{8,9},{10,11},{12,13},{14,15},{16,17},{18,... | collective-permute-start | bytes 33800
  76.9 3.0 %fusion.1 = bf16[16,2816]{1,0:T(8,128)(2,1)S(1)} fusion(bf16[28,2816]{1,0:T(8,128)(2,1)S(1)} %convolution_convert_fusion.2), kind=kCustom, calls=%all-reduce-scatter.1 | all-reduce-scatter fusion | flops 90113 | bytes 248320
  80.0 2.3 %collective-permute-start.16 = (bf16[2,2816]{1,0:T(2,128)(2,1)S(1)}, bf16[2,2816]{1,0:T(2,128)(2,1)S(1)}, u32[]{:S(2)}, u32[]{:S(2)}) collective-permute-start(bf16[2,2816]{1,0:T(2,128)(2,1)S(1)} %slice.55), channel_id=1, source_target_pairs={{0,1},{2,3},{4,5},{6,7},{8,9},{10,11},{12,13},{14,15},{16,17},{18,... | collective-permute-start | bytes 33800
  86.7 16.6 %all-reduce.7.cloned.1.call-done = bf16[28,2,2816]{2,1,0:T(2,128)(2,1)} async-done(((bf16[28,2,2816]{2,1,0:T(2,128)(2,1)}), bf16[28,2,2816]{2,1,0:T(2,128)(2,1)}) %all-reduce.7.cloned.1.call-update) | async-done | bytes 315408
  105.4 4.9 %while.43 = (s32[]{:T(128)}, f32[84,1280]{1,0:T(8,128)S(1)}, s32[]{:T(128)}, bf16[84,1408]{1,0:T(8,128)(2,1)S(1)}, bf16[1408,1280]{1,0:T(8,128)(2,1)}, /*index=5*/s32[]{:T(128)}, s32[]{:T(128)}, s32[]{:T(128)}, s32[]{:T(128)}) while((s32[]{:T(128)}, f32[84,1280]{1,0:T(8,128)S(1)}, s32[]{:T(128)}, bf16[84,1408]{1,0:T(8,128)(2,1)S(1)}, ...), condition=%wide.region_11.12_spmd, body=%wide.region_10.11_spmd.sunk | while | flops 13870086 | bytes 1068179 | solution.py:89
  105.4 1.2 convolution_add_fusion.5
  106.6 1.2 convolution_add_fusion.5
  107.8 1.2 convolution_add_fusion.5
  109.0 1.2 convolution_add_fusion.5
  110.4 20.9 %while.42 = (s32[]{:T(128)}, f32[84,1280]{1,0:T(8,128)S(1)}, s32[]{:T(128)}, bf16[84,1408]{1,0:T(8,128)(2,1)S(1)}, bf16[1408,1280]{1,0:T(8,128)(2,1)}, /*index=5*/s32[]{:T(128)}, s32[]{:T(128)}, s32[]{:T(128)}, s32[]{:T(128)}) while((s32[]{:T(128)}, f32[84,1280]{1,0:T(8,128)S(1)}, s32[]{:T(128)}, bf16[84,1408]{1,0:T(8,128)(2,1)S(1)}, ...), condition=%wide.region_9.10_spmd, body=%wide.region_8.9_spmd.sunk | while | flops 13870086 | bytes 1068179 | solution.py:88
  110.5 1.2 convolution_add_fusion.4
  111.7 1.2 convolution_add_fusion.4
  112.9 1.2 convolution_add_fusion.4
  114.1 1.2 convolution_add_fusion.4
  115.3 1.2 convolution_add_fusion.4
  116.5 1.2 convolution_add_fusion.4
  117.8 1.2 convolution_add_fusion.4
  119.0 1.2 convolution_add_fusion.4
  120.2 1.2 convolution_add_fusion.4
  121.4 1.2 convolution_add_fusion.4
  122.6 1.2 convolution_add_fusion.4
  123.8 1.2 convolution_add_fusion.4
  125.1 1.2 convolution_add_fusion.4
  126.3 1.2 convolution_add_fusion.4
  127.5 1.2 convolution_add_fusion.4
  128.7 1.2 convolution_add_fusion.4
  129.9 1.2 convolution_add_fusion.4
  132.9 1.7 constant_dynamic-slice_fusion
  134.5 1.8 %collective-permute-start = (bf16[3,14,80,4]{2,3,1,0:T(4,128)(2,1)S(1)}, bf16[3,14,80,4]{2,3,1,0:T(4,128)(2,1)S(1)}, u32[]{:S(2)}, u32[]{:S(2)}) collective-permute-start(bf16[3,14,80,4]{2,3,1,0:T(4,128)(2,1)S(1)} %bitcast.196), channel_id=1, source_target_pairs={{0,2},{2,0},{4,6},{6,4},{8,10},{10,8},{12,14},{14,12},{16,18},{18,... | collective-permute-start | bytes 80648 | tf_op jit(solution)/shard_map/ppermute | solution.py:213
  136.4 1.5 collective-permute-start.1
  138.3 1.8 %collective-permute-start.3 = (bf16[3,14,80,4]{2,3,1,0:T(4,128)(2,1)S(1)}, bf16[3,14,80,4]{2,3,1,0:T(4,128)(2,1)S(1)}, u32[]{:S(2)}, u32[]{:S(2)}) collective-permute-start(bf16[3,14,80,4]{2,3,1,0:T(4,128)(2,1)S(1)} %bitcast.193), channel_id=1, source_target_pairs={{0,8},{2,10},{4,12},{6,14},{8,0},{10,2},{12,4},{14,6},{16,24},{18,... | collective-permute-start | bytes 80648 | tf_op jit(solution)/shard_map/ppermute | solution.py:213
  140.2 1.5 collective-permute-start.4
  142.0 2.5 %collective-permute-start.5 = (bf16[3,14,80,4]{2,3,1,0:T(4,128)(2,1)S(1)}, bf16[3,14,80,4]{2,3,1,0:T(4,128)(2,1)S(1)}, u32[]{:S(2)}, u32[]{:S(2)}) collective-permute-start(bf16[3,14,80,4]{2,3,1,0:T(4,128)(2,1)S(1)} %bitcast.191), channel_id=1, source_target_pairs={{0,12},{2,14},{4,8},{6,10},{8,4},{10,6},{12,0},{14,2},{16,28},{18,... | collective-permute-start | bytes 80648 | tf_op jit(solution)/shard_map/ppermute | solution.py:213
  144.8 2.8 %collective-permute-start.7 = (bf16[3,14,80,4]{2,3,1,0:T(4,128)(2,1)S(1)}, bf16[3,14,80,4]{2,3,1,0:T(4,128)(2,1)S(1)}, u32[]{:S(2)}, u32[]{:S(2)}) collective-permute-start(bf16[3,14,80,4]{2,3,1,0:T(4,128)(2,1)S(1)} %bitcast.189), channel_id=1, source_target_pairs={{0,16},{2,18},{4,20},{6,22},{8,24},{10,26},{12,28},{14,30},{16,0},... | collective-permute-start | bytes 80648 | tf_op jit(solution)/shard_map/ppermute | solution.py:213
  147.6 1.5 collective-permute-start.8
  149.1 3.4 %collective-permute-start.9 = (bf16[3,14,80,4]{2,3,1,0:T(4,128)(2,1)S(1)}, bf16[3,14,80,4]{2,3,1,0:T(4,128)(2,1)S(1)}, u32[]{:S(2)}, u32[]{:S(2)}) collective-permute-start(bf16[3,14,80,4]{2,3,1,0:T(4,128)(2,1)S(1)} %bitcast.187), channel_id=1, source_target_pairs={{0,20},{2,22},{4,16},{6,18},{8,28},{10,30},{12,24},{14,26},{16,4},... | collective-permute-start | bytes 80648 | tf_op jit(solution)/shard_map/ppermute | solution.py:213
  152.8 3.7 %collective-permute-start.11 = (bf16[3,14,80,4]{2,3,1,0:T(4,128)(2,1)S(1)}, bf16[3,14,80,4]{2,3,1,0:T(4,128)(2,1)S(1)}, u32[]{:S(2)}, u32[]{:S(2)}) collective-permute-start(bf16[3,14,80,4]{2,3,1,0:T(4,128)(2,1)S(1)} %bitcast.185), channel_id=1, source_target_pairs={{0,24},{2,26},{4,28},{6,30},{8,16},{10,18},{12,20},{14,22},{16,8},... | collective-permute-start | bytes 80648 | tf_op jit(solution)/shard_map/ppermute | solution.py:213
  156.6 1.5 collective-permute-start.12
  158.1 4.3 %collective-permute-start.13 = (bf16[3,14,80,4]{2,3,1,0:T(4,128)(2,1)S(1)}, bf16[3,14,80,4]{2,3,1,0:T(4,128)(2,1)S(1)}, u32[]{:S(2)}, u32[]{:S(2)}) collective-permute-start(bf16[3,14,80,4]{2,3,1,0:T(4,128)(2,1)S(1)} %bitcast.183), channel_id=1, source_target_pairs={{0,28},{2,30},{4,24},{6,26},{8,20},{10,22},{12,16},{14,18},{16,12}... | collective-permute-start | bytes 80648 | tf_op jit(solution)/shard_map/ppermute | solution.py:213
  163.4 2.0 %collective-permute-done.13 = bf16[3,14,80,4]{2,3,1,0:T(4,128)(2,1)S(1)} collective-permute-done((bf16[3,14,80,4]{2,3,1,0:T(4,128)(2,1)S(1)}, bf16[3,14,80,4]{2,3,1,0:T(4,128)(2,1)S(1)}, u32[]{:S(2)}, u32[]{:S(2)}) %collective-permute-start.13) | collective-permute-done | bytes 26912 | tf_op jit(solution)/shard_map/ppermute | solution.py:213
  165.4 4.7 %collective-permute-done.14 = bf16[3,14,80,4]{2,3,1,0:T(4,128)(2,1)S(1)} collective-permute-done((bf16[3,14,80,4]{2,3,1,0:T(4,128)(2,1)S(1)}, bf16[3,14,80,4]{2,3,1,0:T(4,128)(2,1)S(1)}, u32[]{:S(2)}, u32[]{:S(2)}) %collective-permute-start.14) | collective-permute-done | bytes 26912 | tf_op jit(solution)/shard_map/ppermute | solution.py:213
  170.1 1.1 gather_fusion
  (136 shorter events, 27.6 us)
Async XLA Ops:
  7.2 60.9 %copy-start = (f32[28,28]{1,0:T(8,128)S(1)}, f32[28,28]{1,0:T(8,128)}, u32[]{:S(2)}) copy-start(f32[28,28]{1,0:T(8,128)} %param.22) | copy-start | bytes 9412
  7.2 14.3 %copy-start.4 = (s32[16]{0:T(128)S(1)}, s32[16]{0:T(128)}, u32[]{:S(2)}) copy-start(s32[16]{0:T(128)} %param.27) | copy-start | bytes 196
  7.2 17.6 %copy-start.1 = (bf16[3,14,1,2816]{3,1,2,0:T(8,128)(2,1)S(1)}, bf16[3,14,1,2816]{3,1,2,0:T(8,128)(2,1)}, u32[]{:S(2)}) copy-start(bf16[3,14,1,2816]{3,1,2,0:T(8,128)(2,1)} %param.20) | copy-start | bytes 709636
  13.2 28.1 %all-to-all-start = ((bf16[3,14,80,64]{2,1,0,3:T(8,128)(2,1)}), bf16[3,14,80,64]{2,1,0,3:T(8,128)(2,1)S(1)}, u32[]{:S(2)}, u32[]{:S(2)}) async-start(bf16[3,14,80,64]{2,1,0,3:T(8,128)(2,1)} %copy.61), calls=%async_computation | async-start | bytes 1572864 | tf_op jit(solution)/shard_map/all_to_all | solution.py:123
  21.5 81.8 %all-reduce.7.cloned.1.call-start = ((), (), s32[]{:S(2)}) async-start(), calls=%async_computation.1 | async-start | bytes 630784
  67.0 7.6 %copy-start.3 = (u32[32]{0:T(128)S(1)}, u32[32]{0:T(128)}, u32[]{:S(2)}) copy-start(u32[32]{0:T(128)} %constant.144) | copy-start | bytes 388
  67.3 9.2 %copy-start.2 = (f32[28,28]{1,0:T(8,128)S(1)}, f32[28,28]{1,0:T(8,128)}, u32[]{:S(2)}) copy-start(f32[28,28]{1,0:T(8,128)} %param.23) | copy-start | bytes 9412
  67.3 15.0 %copy-start.7 = (f32[28]{0:T(128)S(1)}, f32[28]{0:T(128)}, u32[]{:S(2)}) copy-start(f32[28]{0:T(128)} %param.26) | copy-start | bytes 340
  67.3 16.1 %copy-start.5 = (f32[28,28]{1,0:T(8,128)S(1)}, f32[28,28]{1,0:T(8,128)}, u32[]{:S(2)}) copy-start(f32[28,28]{1,0:T(8,128)} %param.25) | copy-start | bytes 9412
  67.7 16.1 %copy-start.6 = (f32[28,28]{1,0:T(8,128)S(1)}, f32[28,28]{1,0:T(8,128)}, u32[]{:S(2)}) copy-start(f32[28,28]{1,0:T(8,128)} %param.24) | copy-start | bytes 9412
  71.6 4.5 %collective-permute-start.15 = (bf16[2,2816]{1,0:T(2,128)(2,1)S(1)}, bf16[2,2816]{1,0:T(2,128)(2,1)S(1)}, u32[]{:S(2)}, u32[]{:S(2)}) collective-permute-start(bf16[2,2816]{1,0:T(2,128)(2,1)S(1)} %slice.54), channel_id=1, source_target_pairs={{0,1},{2,3},{4,5},{6,7},{8,9},{10,11},{12,13},{14,15},{16,17},{18,... | collective-permute-start | bytes 33800
  80.0 3.1 %collective-permute-start.16 = (bf16[2,2816]{1,0:T(2,128)(2,1)S(1)}, bf16[2,2816]{1,0:T(2,128)(2,1)S(1)}, u32[]{:S(2)}, u32[]{:S(2)}) collective-permute-start(bf16[2,2816]{1,0:T(2,128)(2,1)S(1)} %slice.55), channel_id=1, source_target_pairs={{0,1},{2,3},{4,5},{6,7},{8,9},{10,11},{12,13},{14,15},{16,17},{18,... | collective-permute-start | bytes 33800
  134.5 7.4 %collective-permute-start = (bf16[3,14,80,4]{2,3,1,0:T(4,128)(2,1)S(1)}, bf16[3,14,80,4]{2,3,1,0:T(4,128)(2,1)S(1)}, u32[]{:S(2)}, u32[]{:S(2)}) collective-permute-start(bf16[3,14,80,4]{2,3,1,0:T(4,128)(2,1)S(1)} %bitcast.196), channel_id=1, source_target_pairs={{0,2},{2,0},{4,6},{6,4},{8,10},{10,8},{12,14},{14,12},{16,18},{18,... | collective-permute-start | bytes 80648 | tf_op jit(solution)/shard_map/ppermute | solution.py:213
  136.4 8.0 %collective-permute-start.1 = (bf16[3,14,80,4]{2,3,1,0:T(4,128)(2,1)S(1)}, bf16[3,14,80,4]{2,3,1,0:T(4,128)(2,1)S(1)}, u32[]{:S(2)}, u32[]{:S(2)}) collective-permute-start(bf16[3,14,80,4]{2,3,1,0:T(4,128)(2,1)S(1)} %bitcast.195), channel_id=1, source_target_pairs={{0,4},{2,6},{4,0},{6,2},{8,12},{10,14},{12,8},{14,10},{16,20},{18,... | collective-permute-start | bytes 80648 | tf_op jit(solution)/shard_map/ppermute | solution.py:213
  138.0 6.8 %collective-permute-start.2 = (bf16[3,14,80,4]{2,3,1,0:T(4,128)(2,1)S(1)}, bf16[3,14,80,4]{2,3,1,0:T(4,128)(2,1)S(1)}, u32[]{:S(2)}, u32[]{:S(2)}) collective-permute-start(bf16[3,14,80,4]{2,3,1,0:T(4,128)(2,1)S(1)} %bitcast.194), channel_id=1, source_target_pairs={{0,6},{2,4},{4,2},{6,0},{8,14},{10,12},{12,10},{14,8},{16,22},{18,... | collective-permute-start | bytes 80648 | tf_op jit(solution)/shard_map/ppermute | solution.py:213
  138.3 9.3 %collective-permute-start.3 = (bf16[3,14,80,4]{2,3,1,0:T(4,128)(2,1)S(1)}, bf16[3,14,80,4]{2,3,1,0:T(4,128)(2,1)S(1)}, u32[]{:S(2)}, u32[]{:S(2)}) collective-permute-start(bf16[3,14,80,4]{2,3,1,0:T(4,128)(2,1)S(1)} %bitcast.193), channel_id=1, source_target_pairs={{0,8},{2,10},{4,12},{6,14},{8,0},{10,2},{12,4},{14,6},{16,24},{18,... | collective-permute-start | bytes 80648 | tf_op jit(solution)/shard_map/ppermute | solution.py:213
  140.2 8.9 %collective-permute-start.4 = (bf16[3,14,80,4]{2,3,1,0:T(4,128)(2,1)S(1)}, bf16[3,14,80,4]{2,3,1,0:T(4,128)(2,1)S(1)}, u32[]{:S(2)}, u32[]{:S(2)}) collective-permute-start(bf16[3,14,80,4]{2,3,1,0:T(4,128)(2,1)S(1)} %bitcast.192), channel_id=1, source_target_pairs={{0,10},{2,8},{4,14},{6,12},{8,2},{10,0},{12,6},{14,4},{16,26},{18,... | collective-permute-start | bytes 80648 | tf_op jit(solution)/shard_map/ppermute | solution.py:213
  142.0 10.6 %collective-permute-start.5 = (bf16[3,14,80,4]{2,3,1,0:T(4,128)(2,1)S(1)}, bf16[3,14,80,4]{2,3,1,0:T(4,128)(2,1)S(1)}, u32[]{:S(2)}, u32[]{:S(2)}) collective-permute-start(bf16[3,14,80,4]{2,3,1,0:T(4,128)(2,1)S(1)} %bitcast.191), channel_id=1, source_target_pairs={{0,12},{2,14},{4,8},{6,10},{8,4},{10,6},{12,0},{14,2},{16,28},{18,... | collective-permute-start | bytes 80648 | tf_op jit(solution)/shard_map/ppermute | solution.py:213
  144.4 8.4 %collective-permute-start.6 = (bf16[3,14,80,4]{2,3,1,0:T(4,128)(2,1)S(1)}, bf16[3,14,80,4]{2,3,1,0:T(4,128)(2,1)S(1)}, u32[]{:S(2)}, u32[]{:S(2)}) collective-permute-start(bf16[3,14,80,4]{2,3,1,0:T(4,128)(2,1)S(1)} %bitcast.190), channel_id=1, source_target_pairs={{0,14},{2,12},{4,10},{6,8},{8,6},{10,4},{12,2},{14,0},{16,30},{18,... | collective-permute-start | bytes 80648 | tf_op jit(solution)/shard_map/ppermute | solution.py:213
  144.8 11.8 %collective-permute-start.7 = (bf16[3,14,80,4]{2,3,1,0:T(4,128)(2,1)S(1)}, bf16[3,14,80,4]{2,3,1,0:T(4,128)(2,1)S(1)}, u32[]{:S(2)}, u32[]{:S(2)}) collective-permute-start(bf16[3,14,80,4]{2,3,1,0:T(4,128)(2,1)S(1)} %bitcast.189), channel_id=1, source_target_pairs={{0,16},{2,18},{4,20},{6,22},{8,24},{10,26},{12,28},{14,30},{16,0},... | collective-permute-start | bytes 80648 | tf_op jit(solution)/shard_map/ppermute | solution.py:213
  147.6 10.5 %collective-permute-start.8 = (bf16[3,14,80,4]{2,3,1,0:T(4,128)(2,1)S(1)}, bf16[3,14,80,4]{2,3,1,0:T(4,128)(2,1)S(1)}, u32[]{:S(2)}, u32[]{:S(2)}) collective-permute-start(bf16[3,14,80,4]{2,3,1,0:T(4,128)(2,1)S(1)} %bitcast.188), channel_id=1, source_target_pairs={{0,18},{2,16},{4,22},{6,20},{8,26},{10,24},{12,30},{14,28},{16,2},... | collective-permute-start | bytes 80648 | tf_op jit(solution)/shard_map/ppermute | solution.py:213
  149.1 13.3 %collective-permute-start.9 = (bf16[3,14,80,4]{2,3,1,0:T(4,128)(2,1)S(1)}, bf16[3,14,80,4]{2,3,1,0:T(4,128)(2,1)S(1)}, u32[]{:S(2)}, u32[]{:S(2)}) collective-permute-start(bf16[3,14,80,4]{2,3,1,0:T(4,128)(2,1)S(1)} %bitcast.187), channel_id=1, source_target_pairs={{0,20},{2,22},{4,16},{6,18},{8,28},{10,30},{12,24},{14,26},{16,4},... | collective-permute-start | bytes 80648 | tf_op jit(solution)/shard_map/ppermute | solution.py:213
  152.5 10.2 %collective-permute-start.10 = (bf16[3,14,80,4]{2,3,1,0:T(4,128)(2,1)S(1)}, bf16[3,14,80,4]{2,3,1,0:T(4,128)(2,1)S(1)}, u32[]{:S(2)}, u32[]{:S(2)}) collective-permute-start(bf16[3,14,80,4]{2,3,1,0:T(4,128)(2,1)S(1)} %bitcast.186), channel_id=1, source_target_pairs={{0,22},{2,20},{4,18},{6,16},{8,30},{10,28},{12,26},{14,24},{16,6},... | collective-permute-start | bytes 80648 | tf_op jit(solution)/shard_map/ppermute | solution.py:213
  152.8 9.9 %collective-permute-start.11 = (bf16[3,14,80,4]{2,3,1,0:T(4,128)(2,1)S(1)}, bf16[3,14,80,4]{2,3,1,0:T(4,128)(2,1)S(1)}, u32[]{:S(2)}, u32[]{:S(2)}) collective-permute-start(bf16[3,14,80,4]{2,3,1,0:T(4,128)(2,1)S(1)} %bitcast.185), channel_id=1, source_target_pairs={{0,24},{2,26},{4,28},{6,30},{8,16},{10,18},{12,20},{14,22},{16,8},... | collective-permute-start | bytes 80648 | tf_op jit(solution)/shard_map/ppermute | solution.py:213
  156.6 6.8 %collective-permute-start.12 = (bf16[3,14,80,4]{2,3,1,0:T(4,128)(2,1)S(1)}, bf16[3,14,80,4]{2,3,1,0:T(4,128)(2,1)S(1)}, u32[]{:S(2)}, u32[]{:S(2)}) collective-permute-start(bf16[3,14,80,4]{2,3,1,0:T(4,128)(2,1)S(1)} %bitcast.184), channel_id=1, source_target_pairs={{0,26},{2,24},{4,30},{6,28},{8,18},{10,16},{12,22},{14,20},{16,10}... | collective-permute-start | bytes 80648 | tf_op jit(solution)/shard_map/ppermute | solution.py:213
  158.1 7.3 %collective-permute-start.13 = (bf16[3,14,80,4]{2,3,1,0:T(4,128)(2,1)S(1)}, bf16[3,14,80,4]{2,3,1,0:T(4,128)(2,1)S(1)}, u32[]{:S(2)}, u32[]{:S(2)}) collective-permute-start(bf16[3,14,80,4]{2,3,1,0:T(4,128)(2,1)S(1)} %bitcast.183), channel_id=1, source_target_pairs={{0,28},{2,30},{4,24},{6,26},{8,20},{10,22},{12,16},{14,18},{16,12}... | collective-permute-start | bytes 80648 | tf_op jit(solution)/shard_map/ppermute | solution.py:213
  162.4 7.7 %collective-permute-start.14 = (bf16[3,14,80,4]{2,3,1,0:T(4,128)(2,1)S(1)}, bf16[3,14,80,4]{2,3,1,0:T(4,128)(2,1)S(1)}, u32[]{:S(2)}, u32[]{:S(2)}) collective-permute-start(bf16[3,14,80,4]{2,3,1,0:T(4,128)(2,1)S(1)} %bitcast.182), channel_id=1, source_target_pairs={{0,30},{2,28},{4,26},{6,24},{8,22},{10,20},{12,18},{14,16},{16,14}... | collective-permute-start | bytes 80648 | tf_op jit(solution)/shard_map/ppermute | solution.py:213
Sparse Core Ops, SparseCore 0:
  85.6 17.6 all-reduce.6
